TPU v7x, 32 devices: a whole 2x2x4 slice. The times are simulated.
32 devices in a mesh: rows: 8 (over z, x), feat: 4 (over y, core).
Axes of the slice: x: 2, y: 2, z: 4, core: 2. Of those that a mesh axis runs over, the one named last changes fastest.
Arguments:
- scores: float32 [262144, 64], P(('rows', 'feat'))
- labels: int32 [262144], P('rows'), may hold values from 0 to 63
- bins: int32 [256, 262144], P('feat', 'rows'), may hold values from 0 to 63
- elected: int32 [64, 16], P(None, 'feat'), may hold values from 0 to 255, as said below
Outputs:
- gains: float32 [64, 16, 63], P('rows', 'feat')
Inputs may be any that keep to these rules, and one draw needn't show every extreme that they name: `elected`: for every class and every j < 4, columns j * 4 to (j + 1) * 4 - 1 hold 4 distinct features of the range j * 64 to (j + 1) * 64 - 1.
All inputs are finite; a program needn't handle non-finite values.
Results may differ from a plain program's by a relative error of at most 0.0026.
Values may be sent and summed in bfloat16 or wider, within the bound.
No kernel may reach another device: no remote copies, remote signals or barrier semaphores. Data moves between devices by JAX's collectives and lax.ppermute only.
A program may use at most 64 MiB of HBM per device.

v0:
```python
import math

import jax
import jax.numpy as jnp
from jax import lax
from jax.sharding import PartitionSpec as P

BINS = 64


l2_penalty = 1.0


def grad_columns(scores, labels):
    row_max = jnp.max(scores, axis=1, keepdims=True)
    expon = jnp.exp(scores - row_max)
    probs = expon / jnp.sum(expon, axis=1, keepdims=True)
    target = (labels[:, None] == jnp.arange(scores.shape[1], dtype=jnp.int32)[None, :]).astype(
        jnp.float32
    )
    grad = (probs - target).astype(jnp.bfloat16)
    hess = (probs * (1.0 - probs)).astype(jnp.bfloat16)
    return jnp.concatenate([grad, hess], axis=1)


def split_gains(hist):
    left_g = jnp.cumsum(hist[..., 0], axis=-1)
    left_h = jnp.cumsum(hist[..., 1], axis=-1)
    tot_g = left_g[..., -1:]
    tot_h = left_h[..., -1:]
    right_g = tot_g - left_g
    right_h = tot_h - left_h
    split_gain = 0.5 * (
        left_g * left_g / (left_h + l2_penalty)
        + right_g * right_g / (right_h + l2_penalty)
        - tot_g * tot_g / (tot_h + l2_penalty)
    )
    return split_gain[..., :-1]


def shards(scores, labels, bins, elected):
    feat_group = bins.shape[0]
    own_rows = scores.shape[0]
    classes = scores.shape[1]
    bin_ids = jnp.arange(BINS, dtype=jnp.int32)
    empty = jnp.zeros((feat_group * BINS, 2 * classes), jnp.float32)
    own_labels = lax.dynamic_slice_in_dim(labels, lax.axis_index("feat") * own_rows, own_rows, 0)
    grad_hess = grad_columns(scores, own_labels)
    grad_rows = lax.all_gather(grad_hess, "feat", axis=0, tiled=True)
    piece_rows = grad_rows.shape[0]
    block_len = math.gcd(piece_rows, 2048)

    def step(block_idx, acc):
        block_cols = lax.dynamic_slice_in_dim(grad_rows, block_idx * block_len, block_len, 0)
        bin_codes = lax.dynamic_slice_in_dim(bins, block_idx * block_len, block_len, 1)
        onehot = (bin_codes[:, None, :] == bin_ids[None, :, None]).astype(jnp.bfloat16)
        onehot = onehot.reshape(feat_group * BINS, block_len)
        return acc + jnp.dot(onehot, block_cols, preferred_element_type=jnp.float32)

    hist = lax.fori_loop(0, piece_rows // block_len, step, empty)
    hist_four = hist.reshape(feat_group, BINS, 2, classes)
    local_index = elected - lax.axis_index("feat") * feat_group
    selector = (
        local_index[:, :, None] == jnp.arange(feat_group, dtype=jnp.int32)[None, None, :]
    ).astype(jnp.float32)
    picked_all = jnp.einsum("cef,fbkc->cebk", selector, hist_four, precision=lax.Precision.HIGHEST)
    picked = lax.psum_scatter(picked_all, "rows", scatter_dimension=0, tiled=True)
    return split_gains(picked)


def solution(mesh):
    return jax.shard_map(
        shards,
        mesh=mesh,
        in_specs=(P(("rows", "feat"), None), P("rows"), P("feat", "rows"), P(None, "feat")),
        out_specs=P("rows", "feat", None),
        check_vma=False,
    )
```

profile of v0, /device:TPU:0, one launch (start us, length us, event | category | flops | bytes accessed | tf_op | source)
XLA Modules:
  0.0 417.0 jit_solution(730255659984763662)
XLA Ops:
  6.5 1.9 reduce_max.9
  10.6 1.6 pad_maximum_fusion
  12.9 60.4 %all-gather.2.cloned.1.call-done = bf16[32768,128]{0,1:T(8,128)(2,1)} async-done(((bf16[8192,128]{0,1:T(8,128)(2,1)}), bf16[32768,128]{0,1:T(8,128)(2,1)}) %all-gather.2.cloned.1.call-update) | async-done | bytes 8388624 | tf_op jit(solution)/shard_map/all_gather | solution.py:49
  73.3 247.1 %while.14 = (s32[]{:T(128)}, f32[4096,128]{1,0:T(8,128)S(1)}, s32[64,32768]{1,0:T(8,128)}, bf16[32768,128]{0,1:T(8,128)(2,1)}, s32[]{:T(128)}, /*index=5*/s32[]{:T(128)}, s32[]{:T(128)}, s32[]{:T(128)}) while((s32[]{:T(128)}, f32[4096,128]{1,0:T(8,128)S(1)}, s32[64,32768]{1,0:T(8,128)}, bf16[32768,128]{0,1:T(8,128)(2,1)}, ...), condition=%wide.region_3.0_spmd.clone, body=%wide.region_2.0_spmd.clone.sunk | while | flops 2156920832 | bytes 23134356 | solution.py:60
  74.5 7.1 %bitcast_compare_fusion.2 = pred[4096,2048]{1,0:T(32,128)(4,1)} fusion(s32[4096]{0:T(1024)S(1)} %eq.103, s32[64,2048]{1,0:T(8,128)S(1)} %constant_dynamic-slice_fusion.2), kind=kLoop, calls=%fused_computation.1.clone.1 | loop fusion | flops 8388608 | bytes 8929280 | tf_op jit(solution)/shard_map/while/body/eval_jaxpr/eq | solution.py:56
  81.5 7.2 %convolution_add_fusion.2 = f32[4096,128]{1,0:T(8,128)S(1)} fusion(pred[4096,2048]{1,0:T(32,128)(4,1)} %bitcast_compare_fusion.2, f32[4096,128]{1,0:T(8,128)S(1)} %get-tuple-element.170, pred[]{:T(512)S(6)} %compare.3, bf16[32768,128]{0,1:T(8,128)(2,1)} %get-tuple-element.180, s32[]{:T(128)S(6)} %select_n.14), kind=kOutput, calls=%fused_computation.2.clone.1 | convolution fusion | flops 2148532224 | bytes 13107205 | tf_op jit(solution)/shard_map/while/body/eval_jaxpr/dot_general | solution.py:58
  88.7 1.1 constant_dynamic-slice_fusion.2
  89.9 7.1 %bitcast_compare_fusion.2 = pred[4096,2048]{1,0:T(32,128)(4,1)} fusion(s32[4096]{0:T(1024)S(1)} %eq.103, s32[64,2048]{1,0:T(8,128)S(1)} %constant_dynamic-slice_fusion.2), kind=kLoop, calls=%fused_computation.1.clone.1 | loop fusion | flops 8388608 | bytes 8929280 | tf_op jit(solution)/shard_map/while/body/eval_jaxpr/eq | solution.py:56
  97.0 7.2 %convolution_add_fusion.2 = f32[4096,128]{1,0:T(8,128)S(1)} fusion(pred[4096,2048]{1,0:T(32,128)(4,1)} %bitcast_compare_fusion.2, f32[4096,128]{1,0:T(8,128)S(1)} %get-tuple-element.170, pred[]{:T(512)S(6)} %compare.3, bf16[32768,128]{0,1:T(8,128)(2,1)} %get-tuple-element.180, s32[]{:T(128)S(6)} %select_n.14), kind=kOutput, calls=%fused_computation.2.clone.1 | convolution fusion | flops 2148532224 | bytes 13107205 | tf_op jit(solution)/shard_map/while/body/eval_jaxpr/dot_general | solution.py:58
  104.2 1.1 constant_dynamic-slice_fusion.2
  105.3 7.1 %bitcast_compare_fusion.2 = pred[4096,2048]{1,0:T(32,128)(4,1)} fusion(s32[4096]{0:T(1024)S(1)} %eq.103, s32[64,2048]{1,0:T(8,128)S(1)} %constant_dynamic-slice_fusion.2), kind=kLoop, calls=%fused_computation.1.clone.1 | loop fusion | flops 8388608 | bytes 8929280 | tf_op jit(solution)/shard_map/while/body/eval_jaxpr/eq | solution.py:56
  112.4 7.2 %convolution_add_fusion.2 = f32[4096,128]{1,0:T(8,128)S(1)} fusion(pred[4096,2048]{1,0:T(32,128)(4,1)} %bitcast_compare_fusion.2, f32[4096,128]{1,0:T(8,128)S(1)} %get-tuple-element.170, pred[]{:T(512)S(6)} %compare.3, bf16[32768,128]{0,1:T(8,128)(2,1)} %get-tuple-element.180, s32[]{:T(128)S(6)} %select_n.14), kind=kOutput, calls=%fused_computation.2.clone.1 | convolution fusion | flops 2148532224 | bytes 13107205 | tf_op jit(solution)/shard_map/while/body/eval_jaxpr/dot_general | solution.py:58
  119.6 1.1 constant_dynamic-slice_fusion.2
  120.8 7.1 %bitcast_compare_fusion.2 = pred[4096,2048]{1,0:T(32,128)(4,1)} fusion(s32[4096]{0:T(1024)S(1)} %eq.103, s32[64,2048]{1,0:T(8,128)S(1)} %constant_dynamic-slice_fusion.2), kind=kLoop, calls=%fused_computation.1.clone.1 | loop fusion | flops 8388608 | bytes 8929280 | tf_op jit(solution)/shard_map/while/body/eval_jaxpr/eq | solution.py:56
  127.9 7.2 %convolution_add_fusion.2 = f32[4096,128]{1,0:T(8,128)S(1)} fusion(pred[4096,2048]{1,0:T(32,128)(4,1)} %bitcast_compare_fusion.2, f32[4096,128]{1,0:T(8,128)S(1)} %get-tuple-element.170, pred[]{:T(512)S(6)} %compare.3, bf16[32768,128]{0,1:T(8,128)(2,1)} %get-tuple-element.180, s32[]{:T(128)S(6)} %select_n.14), kind=kOutput, calls=%fused_computation.2.clone.1 | convolution fusion | flops 2148532224 | bytes 13107205 | tf_op jit(solution)/shard_map/while/body/eval_jaxpr/dot_general | solution.py:58
  135.1 1.1 constant_dynamic-slice_fusion.2
  136.2 7.1 %bitcast_compare_fusion.2 = pred[4096,2048]{1,0:T(32,128)(4,1)} fusion(s32[4096]{0:T(1024)S(1)} %eq.103, s32[64,2048]{1,0:T(8,128)S(1)} %constant_dynamic-slice_fusion.2), kind=kLoop, calls=%fused_computation.1.clone.1 | loop fusion | flops 8388608 | bytes 8929280 | tf_op jit(solution)/shard_map/while/body/eval_jaxpr/eq | solution.py:56
  143.3 7.2 %convolution_add_fusion.2 = f32[4096,128]{1,0:T(8,128)S(1)} fusion(pred[4096,2048]{1,0:T(32,128)(4,1)} %bitcast_compare_fusion.2, f32[4096,128]{1,0:T(8,128)S(1)} %get-tuple-element.170, pred[]{:T(512)S(6)} %compare.3, bf16[32768,128]{0,1:T(8,128)(2,1)} %get-tuple-element.180, s32[]{:T(128)S(6)} %select_n.14), kind=kOutput, calls=%fused_computation.2.clone.1 | convolution fusion | flops 2148532224 | bytes 13107205 | tf_op jit(solution)/shard_map/while/body/eval_jaxpr/dot_general | solution.py:58
  150.5 1.1 constant_dynamic-slice_fusion.2
  151.7 7.1 %bitcast_compare_fusion.2 = pred[4096,2048]{1,0:T(32,128)(4,1)} fusion(s32[4096]{0:T(1024)S(1)} %eq.103, s32[64,2048]{1,0:T(8,128)S(1)} %constant_dynamic-slice_fusion.2), kind=kLoop, calls=%fused_computation.1.clone.1 | loop fusion | flops 8388608 | bytes 8929280 | tf_op jit(solution)/shard_map/while/body/eval_jaxpr/eq | solution.py:56
  158.8 7.2 %convolution_add_fusion.2 = f32[4096,128]{1,0:T(8,128)S(1)} fusion(pred[4096,2048]{1,0:T(32,128)(4,1)} %bitcast_compare_fusion.2, f32[4096,128]{1,0:T(8,128)S(1)} %get-tuple-element.170, pred[]{:T(512)S(6)} %compare.3, bf16[32768,128]{0,1:T(8,128)(2,1)} %get-tuple-element.180, s32[]{:T(128)S(6)} %select_n.14), kind=kOutput, calls=%fused_computation.2.clone.1 | convolution fusion | flops 2148532224 | bytes 13107205 | tf_op jit(solution)/shard_map/while/body/eval_jaxpr/dot_general | solution.py:58
  166.0 1.1 constant_dynamic-slice_fusion.2
  167.1 7.1 %bitcast_compare_fusion.2 = pred[4096,2048]{1,0:T(32,128)(4,1)} fusion(s32[4096]{0:T(1024)S(1)} %eq.103, s32[64,2048]{1,0:T(8,128)S(1)} %constant_dynamic-slice_fusion.2), kind=kLoop, calls=%fused_computation.1.clone.1 | loop fusion | flops 8388608 | bytes 8929280 | tf_op jit(solution)/shard_map/while/body/eval_jaxpr/eq | solution.py:56
  174.2 7.2 %convolution_add_fusion.2 = f32[4096,128]{1,0:T(8,128)S(1)} fusion(pred[4096,2048]{1,0:T(32,128)(4,1)} %bitcast_compare_fusion.2, f32[4096,128]{1,0:T(8,128)S(1)} %get-tuple-element.170, pred[]{:T(512)S(6)} %compare.3, bf16[32768,128]{0,1:T(8,128)(2,1)} %get-tuple-element.180, s32[]{:T(128)S(6)} %select_n.14), kind=kOutput, calls=%fused_computation.2.clone.1 | convolution fusion | flops 2148532224 | bytes 13107205 | tf_op jit(solution)/shard_map/while/body/eval_jaxpr/dot_general | solution.py:58
  182.6 7.1 %bitcast_compare_fusion.2 = pred[4096,2048]{1,0:T(32,128)(4,1)} fusion(s32[4096]{0:T(1024)S(1)} %eq.103, s32[64,2048]{1,0:T(8,128)S(1)} %constant_dynamic-slice_fusion.2), kind=kLoop, calls=%fused_computation.1.clone.1 | loop fusion | flops 8388608 | bytes 8929280 | tf_op jit(solution)/shard_map/while/body/eval_jaxpr/eq | solution.py:56
  189.7 7.2 %convolution_add_fusion.2 = f32[4096,128]{1,0:T(8,128)S(1)} fusion(pred[4096,2048]{1,0:T(32,128)(4,1)} %bitcast_compare_fusion.2, f32[4096,128]{1,0:T(8,128)S(1)} %get-tuple-element.170, pred[]{:T(512)S(6)} %compare.3, bf16[32768,128]{0,1:T(8,128)(2,1)} %get-tuple-element.180, s32[]{:T(128)S(6)} %select_n.14), kind=kOutput, calls=%fused_computation.2.clone.1 | convolution fusion | flops 2148532224 | bytes 13107205 | tf_op jit(solution)/shard_map/while/body/eval_jaxpr/dot_general | solution.py:58
  198.0 7.1 %bitcast_compare_fusion.2 = pred[4096,2048]{1,0:T(32,128)(4,1)} fusion(s32[4096]{0:T(1024)S(1)} %eq.103, s32[64,2048]{1,0:T(8,128)S(1)} %constant_dynamic-slice_fusion.2), kind=kLoop, calls=%fused_computation.1.clone.1 | loop fusion | flops 8388608 | bytes 8929280 | tf_op jit(solution)/shard_map/while/body/eval_jaxpr/eq | solution.py:56
  205.1 7.2 %convolution_add_fusion.2 = f32[4096,128]{1,0:T(8,128)S(1)} fusion(pred[4096,2048]{1,0:T(32,128)(4,1)} %bitcast_compare_fusion.2, f32[4096,128]{1,0:T(8,128)S(1)} %get-tuple-element.170, pred[]{:T(512)S(6)} %compare.3, bf16[32768,128]{0,1:T(8,128)(2,1)} %get-tuple-element.180, s32[]{:T(128)S(6)} %select_n.14), kind=kOutput, calls=%fused_computation.2.clone.1 | convolution fusion | flops 2148532224 | bytes 13107205 | tf_op jit(solution)/shard_map/while/body/eval_jaxpr/dot_general | solution.py:58
  213.5 7.1 %bitcast_compare_fusion.2 = pred[4096,2048]{1,0:T(32,128)(4,1)} fusion(s32[4096]{0:T(1024)S(1)} %eq.103, s32[64,2048]{1,0:T(8,128)S(1)} %constant_dynamic-slice_fusion.2), kind=kLoop, calls=%fused_computation.1.clone.1 | loop fusion | flops 8388608 | bytes 8929280 | tf_op jit(solution)/shard_map/while/body/eval_jaxpr/eq | solution.py:56
  220.5 7.2 %convolution_add_fusion.2 = f32[4096,128]{1,0:T(8,128)S(1)} fusion(pred[4096,2048]{1,0:T(32,128)(4,1)} %bitcast_compare_fusion.2, f32[4096,128]{1,0:T(8,128)S(1)} %get-tuple-element.170, pred[]{:T(512)S(6)} %compare.3, bf16[32768,128]{0,1:T(8,128)(2,1)} %get-tuple-element.180, s32[]{:T(128)S(6)} %select_n.14), kind=kOutput, calls=%fused_computation.2.clone.1 | convolution fusion | flops 2148532224 | bytes 13107205 | tf_op jit(solution)/shard_map/while/body/eval_jaxpr/dot_general | solution.py:58
  227.7 1.1 constant_dynamic-slice_fusion.2
  228.9 7.1 %bitcast_compare_fusion.2 = pred[4096,2048]{1,0:T(32,128)(4,1)} fusion(s32[4096]{0:T(1024)S(1)} %eq.103, s32[64,2048]{1,0:T(8,128)S(1)} %constant_dynamic-slice_fusion.2), kind=kLoop, calls=%fused_computation.1.clone.1 | loop fusion | flops 8388608 | bytes 8929280 | tf_op jit(solution)/shard_map/while/body/eval_jaxpr/eq | solution.py:56
  236.0 7.2 %convolution_add_fusion.2 = f32[4096,128]{1,0:T(8,128)S(1)} fusion(pred[4096,2048]{1,0:T(32,128)(4,1)} %bitcast_compare_fusion.2, f32[4096,128]{1,0:T(8,128)S(1)} %get-tuple-element.170, pred[]{:T(512)S(6)} %compare.3, bf16[32768,128]{0,1:T(8,128)(2,1)} %get-tuple-element.180, s32[]{:T(128)S(6)} %select_n.14), kind=kOutput, calls=%fused_computation.2.clone.1 | convolution fusion | flops 2148532224 | bytes 13107205 | tf_op jit(solution)/shard_map/while/body/eval_jaxpr/dot_general | solution.py:58
  244.4 7.1 %bitcast_compare_fusion.2 = pred[4096,2048]{1,0:T(32,128)(4,1)} fusion(s32[4096]{0:T(1024)S(1)} %eq.103, s32[64,2048]{1,0:T(8,128)S(1)} %constant_dynamic-slice_fusion.2), kind=kLoop, calls=%fused_computation.1.clone.1 | loop fusion | flops 8388608 | bytes 8929280 | tf_op jit(solution)/shard_map/while/body/eval_jaxpr/eq | solution.py:56
  251.4 7.2 %convolution_add_fusion.2 = f32[4096,128]{1,0:T(8,128)S(1)} fusion(pred[4096,2048]{1,0:T(32,128)(4,1)} %bitcast_compare_fusion.2, f32[4096,128]{1,0:T(8,128)S(1)} %get-tuple-element.170, pred[]{:T(512)S(6)} %compare.3, bf16[32768,128]{0,1:T(8,128)(2,1)} %get-tuple-element.180, s32[]{:T(128)S(6)} %select_n.14), kind=kOutput, calls=%fused_computation.2.clone.1 | convolution fusion | flops 2148532224 | bytes 13107205 | tf_op jit(solution)/shard_map/while/body/eval_jaxpr/dot_general | solution.py:58
  259.8 7.1 %bitcast_compare_fusion.2 = pred[4096,2048]{1,0:T(32,128)(4,1)} fusion(s32[4096]{0:T(1024)S(1)} %eq.103, s32[64,2048]{1,0:T(8,128)S(1)} %constant_dynamic-slice_fusion.2), kind=kLoop, calls=%fused_computation.1.clone.1 | loop fusion | flops 8388608 | bytes 8929280 | tf_op jit(solution)/shard_map/while/body/eval_jaxpr/eq | solution.py:56
  266.9 7.2 %convolution_add_fusion.2 = f32[4096,128]{1,0:T(8,128)S(1)} fusion(pred[4096,2048]{1,0:T(32,128)(4,1)} %bitcast_compare_fusion.2, f32[4096,128]{1,0:T(8,128)S(1)} %get-tuple-element.170, pred[]{:T(512)S(6)} %compare.3, bf16[32768,128]{0,1:T(8,128)(2,1)} %get-tuple-element.180, s32[]{:T(128)S(6)} %select_n.14), kind=kOutput, calls=%fused_computation.2.clone.1 | convolution fusion | flops 2148532224 | bytes 13107205 | tf_op jit(solution)/shard_map/while/body/eval_jaxpr/dot_general | solution.py:58
  274.1 1.1 constant_dynamic-slice_fusion.2
  275.3 7.1 %bitcast_compare_fusion.2 = pred[4096,2048]{1,0:T(32,128)(4,1)} fusion(s32[4096]{0:T(1024)S(1)} %eq.103, s32[64,2048]{1,0:T(8,128)S(1)} %constant_dynamic-slice_fusion.2), kind=kLoop, calls=%fused_computation.1.clone.1 | loop fusion | flops 8388608 | bytes 8929280 | tf_op jit(solution)/shard_map/while/body/eval_jaxpr/eq | solution.py:56
  282.3 7.2 %convolution_add_fusion.2 = f32[4096,128]{1,0:T(8,128)S(1)} fusion(pred[4096,2048]{1,0:T(32,128)(4,1)} %bitcast_compare_fusion.2, f32[4096,128]{1,0:T(8,128)S(1)} %get-tuple-element.170, pred[]{:T(512)S(6)} %compare.3, bf16[32768,128]{0,1:T(8,128)(2,1)} %get-tuple-element.180, s32[]{:T(128)S(6)} %select_n.14), kind=kOutput, calls=%fused_computation.2.clone.1 | convolution fusion | flops 2148532224 | bytes 13107205 | tf_op jit(solution)/shard_map/while/body/eval_jaxpr/dot_general | solution.py:58
  290.7 7.1 %bitcast_compare_fusion.2 = pred[4096,2048]{1,0:T(32,128)(4,1)} fusion(s32[4096]{0:T(1024)S(1)} %eq.103, s32[64,2048]{1,0:T(8,128)S(1)} %constant_dynamic-slice_fusion.2), kind=kLoop, calls=%fused_computation.1.clone.1 | loop fusion | flops 8388608 | bytes 8929280 | tf_op jit(solution)/shard_map/while/body/eval_jaxpr/eq | solution.py:56
  297.8 7.2 %convolution_add_fusion.2 = f32[4096,128]{1,0:T(8,128)S(1)} fusion(pred[4096,2048]{1,0:T(32,128)(4,1)} %bitcast_compare_fusion.2, f32[4096,128]{1,0:T(8,128)S(1)} %get-tuple-element.170, pred[]{:T(512)S(6)} %compare.3, bf16[32768,128]{0,1:T(8,128)(2,1)} %get-tuple-element.180, s32[]{:T(128)S(6)} %select_n.14), kind=kOutput, calls=%fused_computation.2.clone.1 | convolution fusion | flops 2148532224 | bytes 13107205 | tf_op jit(solution)/shard_map/while/body/eval_jaxpr/dot_general | solution.py:58
  306.1 7.1 %bitcast_compare_fusion.2 = pred[4096,2048]{1,0:T(32,128)(4,1)} fusion(s32[4096]{0:T(1024)S(1)} %eq.103, s32[64,2048]{1,0:T(8,128)S(1)} %constant_dynamic-slice_fusion.2), kind=kLoop, calls=%fused_computation.1.clone.1 | loop fusion | flops 8388608 | bytes 8929280 | tf_op jit(solution)/shard_map/while/body/eval_jaxpr/eq | solution.py:56
  313.2 7.2 %convolution_add_fusion.2 = f32[4096,128]{1,0:T(8,128)S(1)} fusion(pred[4096,2048]{1,0:T(32,128)(4,1)} %bitcast_compare_fusion.2, f32[4096,128]{1,0:T(8,128)S(1)} %get-tuple-element.170, pred[]{:T(512)S(6)} %compare.3, bf16[32768,128]{0,1:T(8,128)(2,1)} %get-tuple-element.180, s32[]{:T(128)S(6)} %select_n.14), kind=kOutput, calls=%fused_computation.2.clone.1 | convolution fusion | flops 2148532224 | bytes 13107205 | tf_op jit(solution)/shard_map/while/body/eval_jaxpr/dot_general | solution.py:58
  320.4 3.7 reshape.18
  324.1 7.5 %copy.25 = f32[64,64,2,64]{1,0,2,3:T(8,128)} copy(f32[64,64,2,64]{3,2,1,0:T(2,128)} %reshape.18) | data formatting | bytes 4194304 | tf_op jit(solution)/shard_map/reshape | solution.py:61
  331.6 4.4 %fusion.8 = f32[64,4,64,2]{2,1,3,0:T(4,128)} fusion(f32[64,64,2,64]{1,0,2,3:T(8,128)} %copy.25, s32[64,4]{1,0:T(8,128)S(1)} %copy.23), kind=kOutput, calls=%fused_computation.16 | convolution fusion | flops 25182208 | bytes 2229248 | tf_op jit(solution)/shard_map/cef,fbkc->cebk/dot_general | solution.py:66
  337.3 69.5 %all-reduce.3.cloned.1.call-done = f32[64,4,64,2]{2,1,3,0:T(4,128)} async-done(((f32[64,4,64,2]{2,1,3,0:T(4,128)}), f32[64,4,64,2]{2,1,3,0:T(4,128)}) %all-reduce.3.cloned.1.call-update) | async-done | bytes 131088
  (65 shorter events, 16.8 us)
Async XLA Ops:
  6.5 2.2 copy-start
  6.5 66.8 %all-gather.2.cloned.1.call-start = ((), (), s32[]{:S(2)}) async-start(), calls=%async_computation | async-start | bytes 10485760 | tf_op jit(solution)/shard_map/all_gather | solution.py:49
  12.1 0.7 copy-start.1
  12.2 394.6 %all-reduce.3.cloned.1.call-start = ((), (), s32[]{:S(2)}) async-start(), calls=%async_computation.1 | async-start | bytes 524288
  331.6 4.4 %copy-start.2 = (u32[32]{0:T(128)S(1)}, u32[32]{0:T(128)}, u32[]{:S(2)}) copy-start(u32[32]{0:T(128)} %constant.57) | copy-start | bytes 388
Sparse Core Ops, SparseCore 0:
  12.3 60.9 all-gather.1
  336.1 70.5 all-reduce.2
where the time goes:
time: 418 us; the launch traced here: 417 us
  waiting for transfers between devices  130 us (31%)
  other arithmetic  120 us (29%)
  matrix products  119 us (28%)
  local copies, waits for them, and re-layouts  33.5 us (8%)
  between operations  14.1 us (3%)
    dot_general x16, matrix products, step(): return acc + jnp.dot(onehot, block_cols, preferred_element_type=jnp.float32)  115 us
    eq x16, other arithmetic, step(): bin_codes[:, None, :] == bin_ids[None, :, None]  113 us
    unnamed x3, waiting for transfers between devices  69.5 us
    all_gather x1, waiting for transfers between devices, shards(): grad_rows = lax.all_gather(grad_hess, 'feat', axis=0, tiled=True)  60.4 us
    dynamic_slice x16, local copies, waits for them, and re-layouts, step(): lax.dynamic_slice_in_dim(bins, block_idx * block_len, block_len, 1)  17.3 us
    reshape x2, local copies, waits for them, and re-layouts, shards(): hist_four = hist.reshape(feat_group, BINS, 2, classes)  11.2 us
  transfers between devices with their start and end apart: 2, of which 2 were waited for; matrix products, arithmetic and copies ran while one was open for 0% of the time, Pallas kernels for 0%

commit v1 on v0

v1 whole, which is shorter than its diff:
```python
import jax
import jax.numpy as jnp
from jax import lax
from jax.experimental import pallas as pl
from jax.experimental.pallas import tpu as pltpu
from jax.sharding import PartitionSpec as P

BINS = 64
LANES = 128
l2_penalty = 1.0

SURE = -1e-30

F8 = jnp.float8_e4m3fn
FULL = 256.0
LOW = 16.0


def rounded(x):
    far = x * 65537.0
    return far - (far - x)


def nudged(code, side, wanted):
    code = rounded(code)
    found = rounded(code + side)
    unit = jnp.abs(code) * (1.25 / 256.0)
    return jnp.where(wanted > found, code + unit, jnp.where(wanted < found, code - unit, code))


def score_kernel(n_blocks, scores_ref, labels_ref, coded_ref, score_slots, label_slot, sems):
    rows = scores_ref.shape[1]
    block = rows // n_blocks
    begin = pl.multiple_of(lax.axis_index("feat") * rows, rows)
    label_copy = pltpu.make_async_copy(labels_ref.at[:, pl.ds(begin, rows)], label_slot, sems.at[n_blocks])
    label_copy.start()
    copies = [
        pltpu.make_async_copy(
            scores_ref.at[:, pl.ds(i * block, block)], score_slots.at[:, pl.ds(i * block, block)], sems.at[i]
        )
        for i in range(n_blocks)
    ]
    for copy in copies:
        copy.start()
    label_copy.wait()
    for i in range(n_blocks):
        copies[i].wait()
        where = pl.ds(i * block, block)
        coded_ref[:, where] = encode(score_slots[:, where], label_slot[:, where]).astype(coded_ref.dtype)


def encode(scores, labels):
    is_label = lax.broadcasted_iota(jnp.int32, scores.shape, 0) == labels
    row_max = jnp.max(scores, axis=0, keepdims=True)
    expon = jnp.exp(scores - row_max)
    probs = expon / jnp.sum(expon, axis=0, keepdims=True)
    top = jnp.max(probs, axis=0, keepdims=True)
    labelled = jnp.sum(jnp.where(is_label, probs, 0.0), axis=0, keepdims=True)
    top_code = nudged(jnp.minimum(top - 1.0, SURE), 1.0, rounded(top))
    label_code = jnp.where(
        labelled > 0.5,
        jnp.minimum(labelled - 1.0, SURE),
        nudged(labelled, -1.0, rounded(labelled - 1.0)),
    )
    return jnp.where(is_label, label_code, jnp.where(probs > 0.5, top_code, probs))


def in_hbm(array):
    return pltpu.with_memory_space_constraint(array, pltpu.HBM)


def score(scores, labels):
    classes, rows = scores.shape
    n_blocks = 4
    far = pl.BlockSpec(memory_space=pltpu.HBM)
    return pl.pallas_call(
        lambda *refs: score_kernel(n_blocks, *refs),
        in_specs=[far, far],
        out_specs=pl.BlockSpec(memory_space=pltpu.VMEM),
        scratch_shapes=[
            pltpu.VMEM((classes, rows), jnp.float32),
            pltpu.VMEM((1, rows), jnp.int32),
            pltpu.SemaphoreType.DMA((n_blocks + 1,)),
        ],
        out_shape=jax.ShapeDtypeStruct((classes, rows), jnp.bfloat16),
        compiler_params=pltpu.CompilerParams(vmem_limit_bytes=48 << 20),
        cost_estimate=pl.CostEstimate(
            flops=10 * rows * classes, bytes_accessed=6 * rows * classes, transcendentals=rows * classes
        ),
    )(in_hbm(scores), in_hbm(labels))


def decode(coded, labels, first_class):
    classes, length = coded.shape
    value = coded.astype(jnp.float32)
    is_label = lax.broadcasted_iota(jnp.int32, (classes, length), 0) + first_class == labels
    above = value < 0.0
    side = jnp.where(above, 1.0, -1.0)
    crossed = is_label != above
    near = jnp.where(crossed, rounded(value + side) - side, value)
    whole = jnp.where(crossed, side, 0.0)
    size = jnp.abs(value)
    return near, whole, near - (size - size * size)


def power_of_two(values):
    largest = jnp.max(jnp.abs(values), axis=1, keepdims=True)
    scale = jnp.ones_like(largest)
    back = jnp.ones_like(largest)
    for power in (16, 8, 4, 2, 1):
        small = largest * scale <= 0.5**power
        scale = jnp.where(small, scale * 2.0**power, scale)
        back = jnp.where(small, back * 0.5**power, back)
    return scale * FULL, back * (1.0 / FULL)


def put_columns(coded_ref, labels, first_class, count, columns_ref, backs_ref):
    classes = coded_ref.shape[0]
    near, whole, square = decode(coded_ref[pl.ds(first_class, count), :], labels, first_class)

    def put(kind, columns, back):
        where = pl.ds(kind * classes + first_class, count)
        columns_ref[where, :] = columns
        backs_ref[where, :] = jnp.broadcast_to(back, (count, backs_ref.shape[1]))

    scale, back = power_of_two(near)
    scaled = near * scale
    high = scaled.astype(F8)
    put(0, high, back)
    put(1, ((scaled - high.astype(jnp.float32)) * LOW).astype(F8), back * (1.0 / LOW))
    scale, back = power_of_two(square)
    put(2, (square * scale).astype(F8), back)
    put(3, whole.astype(F8), jnp.ones_like(back))


def back_row(backs_ref):
    rows, lanes = backs_ref.shape
    sub = lax.broadcasted_iota(jnp.int32, (lanes, lanes), 0)
    diagonal = sub == lax.broadcasted_iota(jnp.int32, (lanes, lanes), 1)
    parts = [
        jnp.sum(jnp.where(diagonal, backs_ref[start : start + lanes, :], 0.0), axis=0, keepdims=True)
        for start in range(0, rows, lanes)
    ]
    return jnp.concatenate(parts, axis=1)


def add_tile(bins_ref, columns_ref, back, sums_ref, first_feature, count, fresh):
    length = bins_ref.shape[1]
    bin_ids = lax.broadcasted_iota(jnp.int32, (BINS, length), 0).astype(jnp.int8)
    one = jnp.ones((BINS, length), F8)
    zero = jnp.zeros((BINS, length), F8)
    parts = []
    for offset in range(count):
        codes = jnp.broadcast_to(bins_ref[pl.ds(first_feature + offset, 1), :], (BINS, length))
        parts.append(jnp.where(codes.astype(jnp.int8) == bin_ids, one, zero))
    added = lax.dot_general(
        jnp.concatenate(parts, axis=0),
        columns_ref[...],
        (((1,), (1,)), ((), ())),
        preferred_element_type=jnp.float32,
    )
    added = added * back
    where = pl.ds(pl.multiple_of(first_feature * BINS, count * BINS), count * BINS)
    if fresh:
        sums_ref[where, :] = added
    else:
        sums_ref[where, :] += added


def hist_kernel(group, length, shifts, n_feat, cores, chained, *refs):
    count = len(shifts)
    elect_ref, bins_ref, labels_ref = refs[:3]
    coded_refs = refs[3 : 3 + count]
    refs = refs[3 + count :]
    if chained:
        before_ref, refs = refs[0], refs[1:]
    out_ref, sums_ref, bin_slots, label_slots, coded_slots = refs[:5]
    columns = refs[5:7]
    backs = refs[7:9]
    bin_sems, label_sems, coded_sems, elect_slot, elect_sem = refs[9:]
    classes, rows = coded_refs[0].shape
    features = bins_ref.shape[0]
    place = lax.axis_index("feat")
    halves = rows // length
    blocks = [(part, half) for part in range(count) for half in range(halves)]

    bin_copies, code_copies = [], []
    for index, (part, half) in enumerate(blocks):
        turn, swapped = shifts[part]
        source = (place - turn * cores + n_feat) % n_feat
        if swapped:
            source = source + 1 - 2 * (source % 2)
        begin = pl.multiple_of(source * rows + half * length, length)
        bin_copies.append(
            pltpu.make_async_copy(
                bins_ref.at[:, pl.ds(begin, length)], bin_slots.at[index % 2], bin_sems.at[index]
            )
        )
        code_copies.append(
            (
                pltpu.make_async_copy(
                    coded_refs[part].at[:, pl.ds(half * length, length)],
                    coded_slots.at[index],
                    coded_sems.at[index],
                ),
                pltpu.make_async_copy(
                    labels_ref.at[:, pl.ds(begin, length)], label_slots.at[index], label_sems.at[index]
                ),
            )
        )
    elect_copy = pltpu.make_async_copy(elect_ref, elect_slot, elect_sem)
    elect_copy.start()
    for copy in code_copies[0]:
        copy.start()
    bin_copies[0].start()
    bin_copies[1].start()
    for pair in code_copies[1:]:
        for copy in pair:
            copy.start()

    tiles = features // group
    turns = 2 if tiles % 2 == 0 and classes % 64 == 0 else 1
    each = classes // turns
    for copy in code_copies[0]:
        copy.wait()
    put_columns(coded_slots.at[0], label_slots[0], 0, classes, columns[0], backs[0])

    for index in range(len(blocks)):
        now, later = index % 2, (index + 1) % 2
        back = back_row(backs[now])
        bin_copies[index].wait()
        more = index + 1 < len(blocks)
        if more:
            for copy in code_copies[index + 1]:
                copy.wait()

        def one_turn(turn, carry):
            for tile in range(tiles // turns):
                feature = (turn * (tiles // turns) + tile) * group
                add_tile(bin_slots.at[now], columns[now], back, sums_ref, feature, group, index == 0)
            if more:
                first = pl.multiple_of(turn * each, each)
                put_columns(
                    coded_slots.at[index + 1], label_slots[index + 1], first, each, columns[later], backs[later]
                )
            return carry

        lax.fori_loop(0, turns, one_turn, 0)
        if index + 2 < len(blocks):
            bin_copies[index + 2].start()

    elect_copy.wait()
    elected = jnp.concatenate([elect_slot[...]] * 4, axis=1) - place * features
    elect = elected.shape[0]

    def pick(feature, picked):
        rows = sums_ref[pl.ds(pl.multiple_of(feature * BINS, BINS), BINS), :]
        return tuple(jnp.where(elected[e : e + 1, :] == feature, rows, picked[e]) for e in range(elect))

    nothing = tuple(jnp.zeros((BINS, 4 * classes), jnp.float32) for _ in range(elect))
    picked = lax.fori_loop(0, features, pick, nothing, unroll=2)
    by_class = jnp.concatenate([part.T for part in picked], axis=1)
    near = by_class[:classes] + by_class[classes : 2 * classes]
    square = by_class[2 * classes : 3 * classes]
    whole = by_class[3 * classes :]
    kinds = (near + whole, near - square)
    owners, _, owned, _ = out_ref.shape
    for owner in range(owners):
        for kind in range(2):
            mine = kinds[kind][owner * owned : (owner + 1) * owned, :]
            out_ref[owner, kind] = before_ref[owner, kind] + mine if chained else mine


def add_hist(before, out_shape, bins, labels, elected, parts, shifts, n_feat, cores):
    features = bins.shape[0]
    classes, rows = parts[0].shape
    length = rows // 2
    count = len(parts)
    blocks = 2 * count
    group = min(features, 16)
    chained = before is not None
    vmem = pl.BlockSpec(memory_space=pltpu.VMEM)
    far = pl.BlockSpec(memory_space=pltpu.HBM)
    near = pl.BlockSpec(memory_space=pl.ANY)
    return pl.pallas_call(
        lambda *refs: hist_kernel(group, length, shifts, n_feat, cores, chained, *refs),
        in_specs=[far, far, far] + [near] * count + [vmem] * chained,
        out_specs=vmem,
        scratch_shapes=[
            pltpu.VMEM((features * BINS, 4 * classes), jnp.float32),
            pltpu.VMEM((2, features, length), jnp.int32),
            pltpu.VMEM((blocks, 1, length), jnp.int32),
            pltpu.VMEM((blocks, classes, length), jnp.bfloat16),
            pltpu.VMEM((4 * classes, length), F8),
            pltpu.VMEM((4 * classes, length), F8),
            pltpu.VMEM((4 * classes, 2 * classes), jnp.float32),
            pltpu.VMEM((4 * classes, 2 * classes), jnp.float32),
            pltpu.SemaphoreType.DMA((blocks,)),
            pltpu.SemaphoreType.DMA((blocks,)),
            pltpu.SemaphoreType.DMA((blocks,)),
            pltpu.VMEM(elected.shape, jnp.int32),
            pltpu.SemaphoreType.DMA,
        ],
        out_shape=jax.ShapeDtypeStruct(out_shape, jnp.float32),
        compiler_params=pltpu.CompilerParams(vmem_limit_bytes=48 << 20),
        cost_estimate=pl.CostEstimate(
            flops=2 * count * rows * features * BINS * 4 * classes,
            bytes_accessed=4 * count * rows * features,
            transcendentals=0,
        ),
    )(in_hbm(elected), in_hbm(bins), in_hbm(labels), *parts, *([before] if chained else []))


def gains_kernel(parts_ref, out_ref):
    hist = parts_ref[0]
    for part in range(1, parts_ref.shape[0]):
        hist = hist + parts_ref[part]
    _, owned, width = hist.shape
    hist = hist.reshape(2 * owned, width)
    lane = lax.broadcasted_iota(jnp.int32, hist.shape, 1) % BINS
    shift = 1
    while shift < BINS:
        hist = hist + jnp.where(lane >= shift, pltpu.roll(hist, shift, 1), 0.0)
        shift *= 2
    for e in range(width // BINS):
        left_g = hist[:owned, e * BINS : (e + 1) * BINS]
        left_h = hist[owned:, e * BINS : (e + 1) * BINS]
        tot_g = left_g[:, BINS - 1 :]
        tot_h = left_h[:, BINS - 1 :]
        right_g = tot_g - left_g
        right_h = tot_h - left_h
        gain = 0.5 * (
            left_g * left_g / (left_h + l2_penalty)
            + right_g * right_g / (right_h + l2_penalty)
            - tot_g * tot_g / (tot_h + l2_penalty)
        )
        out_ref[:, e, :] = gain[:, : BINS - 1]


def shards(axis_sizes, scores, labels, bins, elected):
    n_rows, n_feat = axis_sizes
    own_rows, classes = scores.shape
    features = bins.shape[0]
    elect = elected.shape[1]
    owned = classes // n_rows
    labels = labels[None, :]
    cores = 2 if n_feat % 2 == 0 else 1
    chips = n_feat // cores
    swap = [(i, i ^ 1) for i in range(n_feat)]
    coded = score(scores.T, labels)

    def add(hist, parts, shifts):
        shape = (n_rows, 2, owned, elect * BINS)
        return add_hist(hist, shape, bins, labels, elected.T, parts, shifts, n_feat, cores)

    arrived = []
    for turn in range(1, chips):
        around = [(i, (i + turn * cores) % n_feat) for i in range(n_feat)]
        arrived.append(lax.ppermute(coded, "feat", around))
    if cores == 2:
        hist = add(None, [coded, lax.ppermute(coded, "feat", swap)], [(0, 0), (0, 1)])
    else:
        hist = add(None, [coded], [(0, 0)])
    for turn, part in enumerate(arrived, 1):
        part, hist = lax.optimization_barrier((part, hist))
        mate = lax.ppermute(part, "feat", swap) if cores == 2 else None
        hist = add(hist, [part], [(turn, 0)])
        if cores == 2:
            hist = add(hist, [mate], [(turn, 1)])

    if n_rows > 1:
        hist = lax.all_to_all(hist, "rows", 0, 0, tiled=True)
    return pl.pallas_call(
        gains_kernel,
        out_shape=jax.ShapeDtypeStruct((owned, elect, BINS - 1), jnp.float32),
    )(hist)


def solution(mesh):
    sizes = (mesh.shape["rows"], mesh.shape["feat"])
    return jax.shard_map(
        lambda *arrays: shards(sizes, *arrays),
        mesh=mesh,
        in_specs=(P(("rows", "feat"), None), P("rows"), P("feat", "rows"), P(None, "feat")),
        out_specs=P("rows", "feat", None),
        check_vma=False,
    )
```

time: 418 us -> 78.9 us (0.19)
  waiting for transfers between devices: 130 us -> 0.01 us
  other arithmetic: 120 us -> 0 us
  matrix products: 119 us -> 0 us
  Pallas kernels: 0 us -> 61 us
  local copies, waits for them, and re-layouts: 33.5 us -> 0 us
  blocking collectives: 0 us -> 14.3 us
  between operations: 14.1 us -> 0.05 us
    dot_general x17 -> x0, matrix products: 119 us -> none  [the longest x16 115 us: step(): return acc + jnp.dot(onehot, block_cols, preferred_element_type=jnp.float32)]
    eq x16 -> x0, other arithmetic: 113 us -> none  [step(): bin_codes[:, None, :] == bin_ids[None, :, None]]
    unnamed x3 -> x0, waiting for transfers between devices: 69.5 us -> none
    pallas_call x0 -> x5, Pallas kernels: none -> 61 us  [the longest x3 56 us: add_hist(): pl.pallas_call(lambda *refs: hist_kernel(group, length, shifts, n_feat, c...]
    all_gather x1 -> x0, waiting for transfers between devices: 60.4 us -> none  [shards(): grad_rows = lax.all_gather(grad_hess, 'feat', axis=0, tiled=True)]
    dynamic_slice x17 -> x0, local copies, waits for them, and re-layouts: 18.1 us -> none  [the longest x16 17.3 us: step(): lax.dynamic_slice_in_dim(bins, block_idx * block_len, block_len, 1)]
    all_to_all x0 -> x1, blocking collectives: none -> 14.3 us  [shards(): hist = lax.all_to_all(hist, 'rows', 0, 0, tiled=True)]
    reshape x2 -> x0, local copies, waits for them, and re-layouts: 11.2 us -> none  [shards(): hist_four = hist.reshape(feat_group, BINS, 2, classes)]
  transfers between devices with their start and end apart: 2 -> 3, of which waited for: 2 -> 0; matrix products, arithmetic and copies ran while one was open for 0% -> 0% of each run, Pallas kernels for 0% -> 52%
where the time goes in v1:
time: 78.9 us; the launch traced here: 78.7 us
  Pallas kernels  61 us (77%)
  blocking collectives  14.3 us (18%)
  starting transfers between devices  3.34 us (4%)
    pallas_call x3, Pallas kernels, add_hist(): pl.pallas_call(lambda *refs: hist_kernel(group, length, shifts, n_feat, c...  56 us
    all_to_all x1, blocking collectives, shards(): hist = lax.all_to_all(hist, 'rows', 0, 0, tiled=True)  14.3 us
    pallas_call x1, Pallas kernels, score(): pl.pallas_call(lambda *refs: score_kernel(n_blocks, *refs), in_specs=[far...  2.85 us
    ppermute x1, starting transfers between devices, shards(): arrived.append(lax.ppermute(coded, 'feat', around))  2.59 us
    pallas_call x1, Pallas kernels, shards(): pl.pallas_call(gains_kernel, out_shape=jax.ShapeDtypeStruct((owned, elect...  2.1 us
  transfers between devices with their start and end apart: 3, of which 0 were waited for; matrix products, arithmetic and copies ran while one was open for 0% of the time, Pallas kernels for 52%

profile of v1, /device:TPU:0, one launch (start us, length us, event | category | flops | bytes accessed | tf_op | source)
XLA Modules:
  0.0 78.7 jit_solution(5210399109104714735)
XLA Ops:
  0.0 2.8 %shard_map.46.refs_3_ = bf16[64,8192]{1,0:T(8,128)(2,1)S(1)} custom-call(f32[64,8192]{1,0:T(8,128)} %bitcast.3, s32[1,32768]{1,0:T(1,128)} %bitcast.4), custom_call_target="tpu_custom_call" | custom-call | flops 5242880 | bytes 3145728 | tf_op jit(solution)/shard_map/pallas_call | solution.py:76
  2.9 0.5 collective-permute-start.1
  3.4 2.6 %collective-permute-start = (bf16[64,8192]{1,0:T(8,128)(2,1)S(1)}, bf16[64,8192]{1,0:T(8,128)(2,1)S(1)}, u32[]{:S(2)}, u32[]{:S(2)}) collective-permute-start(bf16[64,8192]{1,0:T(8,128)(2,1)S(1)} %shard_map.46.refs_3_), channel_id=1, source_target_pairs={{0,2},{1,3},{2,0},{3,1},{4,6},{5,7},{6,4},{7,5},{8,10},{9,11},{10,... | collective-permute-start | bytes 3145736 | tf_op jit(solution)/shard_map/ppermute | solution.py:359
  6.0 0.0 collective-permute-done.1.refs_4_
  6.0 26.5 %shard_map.47.refs_4_ = f32[8,2,8,256]{3,2,1,0:T(8,128)S(1)} custom-call(s32[4,64]{1,0:T(4,128)} %bitcast.8, s32[64,32768]{1,0:T(8,128)} %refs_1_.5, s32[1,32768]{1,0:T(1,128)} %bitcast.5, bf16[64,8192]{1,0:T(8,128)(2,1)S(1)} %shard_map.46.refs_3_, bf16[64,8192]{1,0:T(8,128)(2,1)S(1)} %collective-permute-done.1.refs_4_), custom_call_target="tpu_custom_call" | custom-call | flops 34359738368 | bytes 4194304 | tf_op jit(solution)/shard_map/pallas_call | solution.py:285
  32.5 0.0 collective-permute-done.refs_3_
  32.5 0.2 collective-permute-start.2
  32.7 14.8 %shard_map.48.refs_4_ = f32[8,2,8,256]{3,2,1,0:T(8,128)S(1)} custom-call(s32[4,64]{1,0:T(4,128)} %bitcast.9, s32[64,32768]{1,0:T(8,128)} %refs_1_.5, s32[1,32768]{1,0:T(1,128)} %bitcast.6, bf16[64,8192]{1,0:T(8,128)(2,1)S(1)} %collective-permute-done.refs_3_, f32[8,2,8,256]{3,2,1,0:T(8,128)S(1)} %shard_map.47.refs_4_), custom_call_target="tpu_custom_call" | custom-call | flops 17179869184 | bytes 2097152 | tf_op jit(solution)/shard_map/pallas_call | solution.py:285
  47.5 0.0 collective-permute-done.2.refs_3_
  47.5 14.8 %shard_map.49 = f32[8,2,8,256]{3,2,1,0:T(8,128)S(1)} custom-call(s32[4,64]{1,0:T(4,128)} %bitcast.10, s32[64,32768]{1,0:T(8,128)} %refs_1_.5, s32[1,32768]{1,0:T(1,128)} %bitcast.7, bf16[64,8192]{1,0:T(8,128)(2,1)S(1)} %collective-permute-done.2.refs_3_, f32[8,2,8,256]{3,2,1,0:T(8,128)S(1)} %shard_map.48.refs_4_), custom_call_target="tpu_custom_call" | custom-call | flops 17179869184 | bytes 2097152 | tf_op jit(solution)/shard_map/pallas_call | solution.py:285
  62.3 14.3 %all_to_all.5.parts_ref = f32[8,2,8,256]{3,2,1,0:T(8,128)} all-to-all(f32[8,2,8,256]{3,2,1,0:T(8,128)S(1)} %shard_map.49), channel_id=1, replica_groups=mesh['rows'=8,'feat'=4] {'rows'}, dimensions={0} | all-to-all | bytes 262144 | tf_op jit(solution)/shard_map/all_to_all | solution.py:372
  76.5 2.1 %shard_map.50 = f32[8,4,63]{2,1,0:T(4,128)} custom-call(f32[8,2,8,256]{3,2,1,0:T(8,128)} %all_to_all.5.parts_ref), custom_call_target="tpu_custom_call" | custom-call | tf_op jit(solution)/shard_map/pallas_call | solution.py:373
Async XLA Ops:
  2.9 3.1 %collective-permute-start.1 = (bf16[64,8192]{1,0:T(8,128)(2,1)S(1)}, bf16[64,8192]{1,0:T(8,128)(2,1)S(1)}, u32[]{:S(2)}, u32[]{:S(2)}) collective-permute-start(bf16[64,8192]{1,0:T(8,128)(2,1)S(1)} %shard_map.46.refs_3_), channel_id=1, source_target_pairs={{0,1},{1,0},{2,3},{3,2},{4,5},{5,4},{6,7},{7,6},{8,9},{9,8},{10,11... | collective-permute-start | bytes 3145736 | tf_op jit(solution)/shard_map/ppermute | solution.py:361
  3.4 29.1 %collective-permute-start = (bf16[64,8192]{1,0:T(8,128)(2,1)S(1)}, bf16[64,8192]{1,0:T(8,128)(2,1)S(1)}, u32[]{:S(2)}, u32[]{:S(2)}) collective-permute-start(bf16[64,8192]{1,0:T(8,128)(2,1)S(1)} %shard_map.46.refs_3_), channel_id=1, source_target_pairs={{0,2},{1,3},{2,0},{3,1},{4,6},{5,7},{6,4},{7,5},{8,10},{9,11},{10,... | collective-permute-start | bytes 3145736 | tf_op jit(solution)/shard_map/ppermute | solution.py:359
  32.5 15.0 %collective-permute-start.2 = (bf16[64,8192]{1,0:T(8,128)(2,1)S(1)}, bf16[64,8192]{1,0:T(8,128)(2,1)S(1)}, u32[]{:S(2)}, u32[]{:S(2)}) collective-permute-start(bf16[64,8192]{1,0:T(8,128)(2,1)S(1)} %collective-permute-done.refs_3_), channel_id=1, source_target_pairs={{0,1},{1,0},{2,3},{3,2},{4,5},{5,4},{6,7},{7,6},{8,9},{9,8},{10,11... | collective-permute-start | bytes 3145736 | tf_op jit(solution)/shard_map/ppermute | solution.py:366

commit v2 on v1

--- a/solution.py
+++ b/solution.py
@@ -83,7 +83,7 @@
             pltpu.SemaphoreType.DMA((n_blocks + 1,)),
         ],
         out_shape=jax.ShapeDtypeStruct((classes, rows), jnp.bfloat16),
-        compiler_params=pltpu.CompilerParams(vmem_limit_bytes=48 << 20),
+        compiler_params=pltpu.CompilerParams(vmem_limit_bytes=36 << 20),
         cost_estimate=pl.CostEstimate(
             flops=10 * rows * classes, bytes_accessed=6 * rows * classes, transcendentals=rows * classes
         ),
@@ -92,26 +92,27 @@
 
 def decode(coded, labels, first_class):
     classes, length = coded.shape
-    value = coded.astype(jnp.float32)
-    is_label = lax.broadcasted_iota(jnp.int32, (classes, length), 0) + first_class == labels
-    above = value < 0.0
-    side = jnp.where(above, 1.0, -1.0)
+    kind = coded.dtype
+    class_ids = (lax.broadcasted_iota(jnp.int32, (classes, length), 0) + first_class).astype(kind)
+    is_label = class_ids == labels.astype(kind)
+    zero, one = jnp.zeros_like(coded), jnp.ones_like(coded)
+    above = coded < zero
+    side = jnp.where(above, one, -one)
     crossed = is_label != above
-    near = jnp.where(crossed, rounded(value + side) - side, value)
-    whole = jnp.where(crossed, side, 0.0)
-    size = jnp.abs(value)
-    return near, whole, near - (size - size * size)
+    near = jnp.where(crossed, (coded + side) - side, coded)
+    whole = jnp.where(crossed, side, zero)
+    return near, whole, (near - jnp.abs(coded)) + coded * coded
 
 
 def power_of_two(values):
-    largest = jnp.max(jnp.abs(values), axis=1, keepdims=True)
+    largest = jnp.max(jnp.abs(values), axis=1, keepdims=True).astype(jnp.float32)
     scale = jnp.ones_like(largest)
     back = jnp.ones_like(largest)
     for power in (16, 8, 4, 2, 1):
         small = largest * scale <= 0.5**power
         scale = jnp.where(small, scale * 2.0**power, scale)
         back = jnp.where(small, back * 0.5**power, back)
-    return scale * FULL, back * (1.0 / FULL)
+    return (scale * FULL).astype(values.dtype), back * (1.0 / FULL)
 
 
 def put_columns(coded_ref, labels, first_class, count, columns_ref, backs_ref):
@@ -127,7 +128,7 @@
     scaled = near * scale
     high = scaled.astype(F8)
     put(0, high, back)
-    put(1, ((scaled - high.astype(jnp.float32)) * LOW).astype(F8), back * (1.0 / LOW))
+    put(1, ((scaled - high.astype(scaled.dtype)) * LOW).astype(F8), back * (1.0 / LOW))
     scale, back = power_of_two(square)
     put(2, (square * scale).astype(F8), back)
     put(3, whole.astype(F8), jnp.ones_like(back))
@@ -146,13 +147,17 @@
 
 def add_tile(bins_ref, columns_ref, back, sums_ref, first_feature, count, fresh):
     length = bins_ref.shape[1]
-    bin_ids = lax.broadcasted_iota(jnp.int32, (BINS, length), 0).astype(jnp.int8)
-    one = jnp.ones((BINS, length), F8)
-    zero = jnp.zeros((BINS, length), F8)
+    rows = BINS // 2
+    bin_ids = lax.broadcasted_iota(jnp.int32, (rows, length), 0)
+    low_ids, high_ids = bin_ids.astype(jnp.int8), (bin_ids + rows).astype(jnp.int8)
+    one = jnp.ones((rows, length), F8)
+    zero = jnp.zeros((rows, length), F8)
     parts = []
     for offset in range(count):
-        codes = jnp.broadcast_to(bins_ref[pl.ds(first_feature + offset, 1), :], (BINS, length))
-        parts.append(jnp.where(codes.astype(jnp.int8) == bin_ids, one, zero))
+        codes = jnp.broadcast_to(bins_ref[pl.ds(first_feature + offset, 1), :], (rows, length))
+        codes = codes.astype(jnp.int8)
+        parts.append(jnp.where(codes == low_ids, one, zero))
+        parts.append(jnp.where(codes == high_ids, one, zero))
     added = lax.dot_general(
         jnp.concatenate(parts, axis=0),
         columns_ref[...],
@@ -167,17 +172,19 @@
         sums_ref[where, :] += added
 
 
-def hist_kernel(group, length, shifts, n_feat, cores, chained, *refs):
+def hist_kernel(group, length, shifts, n_feat, cores, chained, final, *refs):
     count = len(shifts)
     elect_ref, bins_ref, labels_ref = refs[:3]
     coded_refs = refs[3 : 3 + count]
     refs = refs[3 + count :]
-    if chained:
-        before_ref, refs = refs[0], refs[1:]
-    out_ref, sums_ref, bin_slots, label_slots, coded_slots = refs[:5]
-    columns = refs[5:7]
-    backs = refs[7:9]
-    bin_sems, label_sems, coded_sems, elect_slot, elect_sem = refs[9:]
+    refs = refs[1:] if chained else refs
+    sums_ref, refs = refs[0], refs[1:]
+    if final:
+        out_ref, refs = refs[0], refs[1:]
+    bin_slots, label_slots, coded_slots = refs[:3]
+    columns = refs[3:5]
+    backs = refs[5:7]
+    bin_sems, label_sems, coded_sems, elect_slot, elect_sem = refs[7:]
     classes, rows = coded_refs[0].shape
     features = bins_ref.shape[0]
     place = lax.axis_index("feat")
@@ -208,8 +215,9 @@
                 ),
             )
         )
-    elect_copy = pltpu.make_async_copy(elect_ref, elect_slot, elect_sem)
-    elect_copy.start()
+    if final:
+        elect_copy = pltpu.make_async_copy(elect_ref, elect_slot, elect_sem)
+        elect_copy.start()
     for copy in code_copies[0]:
         copy.start()
     bin_copies[0].start()
@@ -230,6 +238,7 @@
         back = back_row(backs[now])
         bin_copies[index].wait()
         more = index + 1 < len(blocks)
+        fresh = index == 0 and not chained
         if more:
             for copy in code_copies[index + 1]:
                 copy.wait()
@@ -237,7 +246,7 @@
         def one_turn(turn, carry):
             for tile in range(tiles // turns):
                 feature = (turn * (tiles // turns) + tile) * group
-                add_tile(bin_slots.at[now], columns[now], back, sums_ref, feature, group, index == 0)
+                add_tile(bin_slots.at[now], columns[now], back, sums_ref, feature, group, fresh)
             if more:
                 first = pl.multiple_of(turn * each, each)
                 put_columns(
@@ -249,6 +258,8 @@
         if index + 2 < len(blocks):
             bin_copies[index + 2].start()
 
+    if not final:
+        return
     elect_copy.wait()
     elected = jnp.concatenate([elect_slot[...]] * 4, axis=1) - place * features
     elect = elected.shape[0]
@@ -268,7 +279,7 @@
     for owner in range(owners):
         for kind in range(2):
             mine = kinds[kind][owner * owned : (owner + 1) * owned, :]
-            out_ref[owner, kind] = before_ref[owner, kind] + mine if chained else mine
+            out_ref[owner, kind] = mine
 
 
 def add_hist(before, out_shape, bins, labels, elected, parts, shifts, n_feat, cores):
@@ -279,15 +290,17 @@
     blocks = 2 * count
     group = min(features, 16)
     chained = before is not None
+    final = out_shape is not None
     vmem = pl.BlockSpec(memory_space=pltpu.VMEM)
     far = pl.BlockSpec(memory_space=pltpu.HBM)
     near = pl.BlockSpec(memory_space=pl.ANY)
-    return pl.pallas_call(
-        lambda *refs: hist_kernel(group, length, shifts, n_feat, cores, chained, *refs),
+    sums = jax.ShapeDtypeStruct((features * BINS, 4 * classes), jnp.float32)
+    out = jax.ShapeDtypeStruct(out_shape, jnp.float32) if final else None
+    result = pl.pallas_call(
+        lambda *refs: hist_kernel(group, length, shifts, n_feat, cores, chained, final, *refs),
         in_specs=[far, far, far] + [near] * count + [vmem] * chained,
-        out_specs=vmem,
+        out_specs=[vmem, vmem] if final else [vmem],
         scratch_shapes=[
-            pltpu.VMEM((features * BINS, 4 * classes), jnp.float32),
             pltpu.VMEM((2, features, length), jnp.int32),
             pltpu.VMEM((blocks, 1, length), jnp.int32),
             pltpu.VMEM((blocks, classes, length), jnp.bfloat16),
@@ -301,14 +314,16 @@
             pltpu.VMEM(elected.shape, jnp.int32),
             pltpu.SemaphoreType.DMA,
         ],
-        out_shape=jax.ShapeDtypeStruct(out_shape, jnp.float32),
-        compiler_params=pltpu.CompilerParams(vmem_limit_bytes=48 << 20),
+        out_shape=[sums, out] if final else [sums],
+        input_output_aliases={3 + count: 0} if chained else {},
+        compiler_params=pltpu.CompilerParams(vmem_limit_bytes=36 << 20),
         cost_estimate=pl.CostEstimate(
             flops=2 * count * rows * features * BINS * 4 * classes,
             bytes_accessed=4 * count * rows * features,
             transcendentals=0,
         ),
     )(in_hbm(elected), in_hbm(bins), in_hbm(labels), *parts, *([before] if chained else []))
+    return result[-1]
 
 
 def gains_kernel(parts_ref, out_ref):
@@ -349,8 +364,8 @@
     swap = [(i, i ^ 1) for i in range(n_feat)]
     coded = score(scores.T, labels)
 
-    def add(hist, parts, shifts):
-        shape = (n_rows, 2, owned, elect * BINS)
+    def add(hist, parts, shifts, last):
+        shape = (n_rows, 2, owned, elect * BINS) if last else None
         return add_hist(hist, shape, bins, labels, elected.T, parts, shifts, n_feat, cores)
 
     arrived = []
@@ -358,15 +373,17 @@
         around = [(i, (i + turn * cores) % n_feat) for i in range(n_feat)]
         arrived.append(lax.ppermute(coded, "feat", around))
     if cores == 2:
-        hist = add(None, [coded, lax.ppermute(coded, "feat", swap)], [(0, 0), (0, 1)])
+        mate = lax.ppermute(coded, "feat", swap)
+        hist = add(None, [coded, mate], [(0, 0), (0, 1)], chips == 1)
     else:
-        hist = add(None, [coded], [(0, 0)])
+        hist = add(None, [coded], [(0, 0)], chips == 1)
     for turn, part in enumerate(arrived, 1):
+        last = turn == chips - 1
         part, hist = lax.optimization_barrier((part, hist))
         mate = lax.ppermute(part, "feat", swap) if cores == 2 else None
-        hist = add(hist, [part], [(turn, 0)])
+        hist = add(hist, [part], [(turn, 0)], last and cores == 1)
         if cores == 2:
-            hist = add(hist, [mate], [(turn, 1)])
+            hist = add(hist, [mate], [(turn, 1)], last)
 
     if n_rows > 1:
         hist = lax.all_to_all(hist, "rows", 0, 0, tiled=True)

time: 78.9 us -> 72 us (0.913)
  Pallas kernels: 61 us -> 54.1 us
  waiting for transfers between devices: 0.01 us -> 0.8 us
    pallas_call x3, Pallas kernels: 56 us -> 49.2 us  [add_hist(): pl.pallas_call(lambda *refs: hist_kernel(group, length, shifts, n_feat, c...]
  transfers between devices with their start and end apart: 3 -> 3, of which waited for: 0 -> 1; matrix products, arithmetic and copies ran while one was open for 0% -> 0% of each run, Pallas kernels for 52% -> 49%
where the time goes in v2:
time: 72 us; the launch traced here: 71.8 us
  Pallas kernels  54.1 us (75%)
  blocking collectives  13.7 us (19%)
  starting transfers between devices  3.11 us (4%)
  waiting for transfers between devices  0.8 us (1%)
    pallas_call x3, Pallas kernels, add_hist(): pl.pallas_call(lambda *refs: hist_kernel(group, length, shifts, n_feat, c...  49.2 us
    all_to_all x1, blocking collectives, shards(): hist = lax.all_to_all(hist, 'rows', 0, 0, tiled=True)  13.7 us
    pallas_call x1, Pallas kernels, score(): pl.pallas_call(lambda *refs: score_kernel(n_blocks, *refs), in_specs=[far...  2.85 us
    ppermute x1, starting transfers between devices, shards(): arrived.append(lax.ppermute(coded, 'feat', around))  2.59 us
    pallas_call x1, Pallas kernels, shards(): pl.pallas_call(gains_kernel, out_shape=jax.ShapeDtypeStruct((owned, elect...  2.1 us
  transfers between devices with their start and end apart: 3, of which 1 were waited for; matrix products, arithmetic and copies ran while one was open for 0% of the time, Pallas kernels for 49%

profile of v2, /device:TPU:0, one launch (start us, length us, event | category | flops | bytes accessed | tf_op | source)
XLA Modules:
  0.0 71.8 jit_solution(11485703375618885829)
XLA Ops:
  0.0 2.8 %shard_map.46.refs_3_ = bf16[64,8192]{1,0:T(8,128)(2,1)S(1)} custom-call(f32[64,8192]{1,0:T(8,128)} %bitcast.3, s32[1,32768]{1,0:T(1,128)} %bitcast.4), custom_call_target="tpu_custom_call" | custom-call | flops 5242880 | bytes 3145728 | tf_op jit(solution)/shard_map/pallas_call | solution.py:76
  2.9 0.5 collective-permute-start.1
  3.4 2.6 %collective-permute-start = (bf16[64,8192]{1,0:T(8,128)(2,1)S(1)}, bf16[64,8192]{1,0:T(8,128)(2,1)S(1)}, u32[]{:S(2)}, u32[]{:S(2)}) collective-permute-start(bf16[64,8192]{1,0:T(8,128)(2,1)S(1)} %shard_map.46.refs_3_), channel_id=1, source_target_pairs={{0,2},{1,3},{2,0},{3,1},{4,6},{5,7},{6,4},{7,5},{8,10},{9,11},{10,... | collective-permute-start | bytes 3145736 | tf_op jit(solution)/shard_map/ppermute | solution.py:374
  6.0 0.0 collective-permute-done.1.refs_4_
  6.0 23.0 %shard_map.47.refs_4_ = f32[4096,256]{1,0:T(8,128)S(1)} custom-call(s32[4,64]{1,0:T(4,128)} %bitcast.8, s32[64,32768]{1,0:T(8,128)} %refs_1_.5, s32[1,32768]{1,0:T(1,128)} %bitcast.5, bf16[64,8192]{1,0:T(8,128)(2,1)S(1)} %shard_map.46.refs_3_, bf16[64,8192]{1,0:T(8,128)(2,1)S(1)} %collective-permute-done.1.refs_4_), custom_call_target="tpu_custom_call" | custom-call | flops 34359738368 | bytes 4194304 | tf_op jit(solution)/shard_map/pallas_call | solution.py:299
  28.9 0.8 %collective-permute-done.refs_3_ = bf16[64,8192]{1,0:T(8,128)(2,1)S(1)} collective-permute-done((bf16[64,8192]{1,0:T(8,128)(2,1)S(1)}, bf16[64,8192]{1,0:T(8,128)(2,1)S(1)}, u32[]{:S(2)}, u32[]{:S(2)}) %collective-permute-start) | collective-permute-done | bytes 1048608 | tf_op jit(solution)/shard_map/ppermute | solution.py:374
  29.7 0.0 collective-permute-start.2
  29.7 12.2 %shard_map.48.refs_4_ = f32[4096,256]{1,0:T(8,128)S(1)} custom-call(s32[4,64]{1,0:T(4,128)} %bitcast.9, s32[64,32768]{1,0:T(8,128)} %refs_1_.5, s32[1,32768]{1,0:T(1,128)} %bitcast.6, bf16[64,8192]{1,0:T(8,128)(2,1)S(1)} %collective-permute-done.refs_3_, f32[4096,256]{1,0:T(8,128)S(1)} %shard_map.47.refs_4_), custom_call_target="tpu_custom_call", output_to_operand_aliasing={{}: (4, {})} | custom-call | flops 17179869184 | bytes 2097152 | tf_op jit(solution)/shard_map/pallas_call | solution.py:299
  42.0 0.0 collective-permute-done.2.refs_3_
  42.0 14.0 %shard_map.49 = (f32[4096,256]{1,0:T(8,128)S(1)}, f32[8,2,8,256]{3,2,1,0:T(8,128)S(1)}) custom-call(s32[4,64]{1,0:T(4,128)} %bitcast.10, s32[64,32768]{1,0:T(8,128)} %refs_1_.5, s32[1,32768]{1,0:T(1,128)} %bitcast.7, bf16[64,8192]{1,0:T(8,128)(2,1)S(1)} %collective-permute-done.2.refs_3_, ...), custom_call_target="tpu_custom_call", output_to_operand_aliasing={{0}: (4, {})} | custom-call | flops 17179869184 | bytes 2097152 | tf_op jit(solution)/shard_map/pallas_call | solution.py:299
  56.0 13.7 %all_to_all.5.parts_ref = f32[8,2,8,256]{3,2,1,0:T(8,128)} all-to-all(f32[8,2,8,256]{3,2,1,0:T(8,128)S(1)} %get-tuple-element.10), channel_id=1, replica_groups=mesh['rows'=8,'feat'=4] {'rows'}, dimensions={0} | all-to-all | bytes 262144 | tf_op jit(solution)/shard_map/all_to_all | solution.py:389
  69.7 2.1 %shard_map.50 = f32[8,4,63]{2,1,0:T(4,128)} custom-call(f32[8,2,8,256]{3,2,1,0:T(8,128)} %all_to_all.5.parts_ref), custom_call_target="tpu_custom_call" | custom-call | tf_op jit(solution)/shard_map/pallas_call | solution.py:390
Async XLA Ops:
  2.9 3.1 %collective-permute-start.1 = (bf16[64,8192]{1,0:T(8,128)(2,1)S(1)}, bf16[64,8192]{1,0:T(8,128)(2,1)S(1)}, u32[]{:S(2)}, u32[]{:S(2)}) collective-permute-start(bf16[64,8192]{1,0:T(8,128)(2,1)S(1)} %shard_map.46.refs_3_), channel_id=1, source_target_pairs={{0,1},{1,0},{2,3},{3,2},{4,5},{5,4},{6,7},{7,6},{8,9},{9,8},{10,11... | collective-permute-start | bytes 3145736 | tf_op jit(solution)/shard_map/ppermute | solution.py:376
  3.4 26.3 %collective-permute-start = (bf16[64,8192]{1,0:T(8,128)(2,1)S(1)}, bf16[64,8192]{1,0:T(8,128)(2,1)S(1)}, u32[]{:S(2)}, u32[]{:S(2)}) collective-permute-start(bf16[64,8192]{1,0:T(8,128)(2,1)S(1)} %shard_map.46.refs_3_), channel_id=1, source_target_pairs={{0,2},{1,3},{2,0},{3,1},{4,6},{5,7},{6,4},{7,5},{8,10},{9,11},{10,... | collective-permute-start | bytes 3145736 | tf_op jit(solution)/shard_map/ppermute | solution.py:374
  29.7 12.3 %collective-permute-start.2 = (bf16[64,8192]{1,0:T(8,128)(2,1)S(1)}, bf16[64,8192]{1,0:T(8,128)(2,1)S(1)}, u32[]{:S(2)}, u32[]{:S(2)}) collective-permute-start(bf16[64,8192]{1,0:T(8,128)(2,1)S(1)} %collective-permute-done.refs_3_), channel_id=1, source_target_pairs={{0,1},{1,0},{2,3},{3,2},{4,5},{5,4},{6,7},{7,6},{8,9},{9,8},{10,11... | collective-permute-start | bytes 3145736 | tf_op jit(solution)/shard_map/ppermute | solution.py:383
